TPU v7x, 128 devices: a whole 4x4x4 slice. The times are simulated.
128 devices in a mesh: row: 8 (over y, core), col: 16 (over x, z).
Axes of the slice: x: 4, y: 4, z: 4, core: 2. Of those that a mesh axis runs over, the one named last changes fastest.
Arguments:
- atoms: bfloat16 [16384, 128], P(('row', 'col')), may hold values from -6 to 6
- pair: bfloat16 [128, 2048, 2048], P(None, 'row', 'col'), may hold values from -6 to 6
- token_atoms: int32 [2048], replicated, may hold values from 1 to 24, as said below
- attn_bias: float32 [512, 4, 32, 128], P(('row', 'col')), may hold values from -8 to 320
- w_attn: bfloat16 [128, 512], replicated, may hold values from -0.5 to 0.5
- w_attn_out: bfloat16 [128, 128], replicated, may hold values from -0.5 to 0.5
- w_single: bfloat16 [128, 384], replicated, may hold values from -0.5 to 0.5
- w_pair_left: bfloat16 [384, 128], replicated, may hold values from -0.3125 to 0.3125
- w_pair_right: bfloat16 [384, 128], replicated, may hold values from -0.3125 to 0.3125
- w_atom_back: bfloat16 [384, 128], replicated, may hold values from -0.3125 to 0.3125
- w_tri_in: bfloat16 [128, 512], replicated, may hold values from -0.5 to 0.5
- w_tri_gate: bfloat16 [128, 128], replicated, may hold values from -0.5 to 0.5
- w_tri_out: bfloat16 [128, 128], replicated, may hold values from -0.5 to 0.5
Outputs:
- atoms_out: bfloat16 [16384, 128], P(('row', 'col'))
- pair_out: bfloat16 [128, 2048, 2048], P(None, 'row', 'col')
Inputs may be any that keep to these rules, and one draw needn't show every extreme that they name: `token_atoms`: entries sum to 16384; the last 1280 tokens hold one atom each; the largest is exactly 24.
All inputs are finite; a program needn't handle non-finite values.
Results may differ from a plain program's by a relative error of at most 0.006.
Values may be sent and summed in bfloat16 or wider, within the bound.
No kernel may reach another device: no remote copies, remote signals or barrier semaphores. Data moves between devices by JAX's collectives and lax.ppermute only.
A program may use at most 192 MiB of HBM per device.

v0:
```python
import math

import jax
import jax.numpy as jnp
from jax import lax
from jax.sharding import PartitionSpec as P

HEADS = 4
QBLOCK = 32
KWIN = 128


epsilon = 1e-05


def with_halo(array, sides, width):
    for axis, dim in sides:
        peers, length = (lax.axis_size(axis), array.shape[dim])
        up = [(i, (i + 1) % peers) for i in range(peers - 1)]
        down = [(j, i) for i, j in up]
        last = lax.slice_in_dim(array, length - width, length, axis=dim)
        initial = lax.slice_in_dim(array, 0, width, axis=dim)
        before = lax.ppermute(last, axis, up)
        after = lax.ppermute(initial, axis, down)
        array = jnp.concatenate([before, array, after], axis=dim)
    return array


def layer_norm(values, along):
    average = jnp.mean(values, axis=along, keepdims=True)
    centred = values - average
    variance = jnp.mean(centred * centred, axis=along, keepdims=True)
    return centred * lax.rsqrt(variance + epsilon)


def on_device(
    atoms,
    pair,
    token_atoms,
    attn_bias,
    w_attn,
    w_attn_out,
    w_single,
    w_pair_left,
    w_pair_right,
    w_atom_back,
    w_tri_in,
    w_tri_gate,
    w_tri_out,
):
    atom_count = atoms.shape[0]
    atom_width = atoms.shape[1]
    head_dim = atom_width // HEADS
    margin = (KWIN - QBLOCK) // 2
    devices = lax.axis_size(("row", "col"))
    row_devices = lax.axis_size("row")
    col_devices = lax.axis_size("col")
    device_index = lax.axis_index(("row", "col"))
    tokens = token_atoms.shape[0]
    channels = pair.shape[0]
    tile_rows = pair.shape[1]
    tile_cols = pair.shape[2]
    per_channel = channels // devices
    normed = layer_norm(atoms.astype(jnp.float32), 1).astype(jnp.bfloat16)
    projected = jnp.dot(normed, w_attn, preferred_element_type=jnp.float32)
    queries = projected[:, :atom_width].astype(jnp.bfloat16)
    key_value = projected[:, atom_width : 3 * atom_width].astype(jnp.bfloat16)
    gating = jax.nn.sigmoid(projected[:, 3 * atom_width :])
    padded = with_halo(key_value, ((("row", "col"), 0),), margin)
    blocks = atom_count // QBLOCK
    key_index = (
        QBLOCK * jnp.arange(blocks, dtype=jnp.int32)[:, None]
        + jnp.arange(KWIN, dtype=jnp.int32)[None, :]
    )
    windows = padded[key_index]
    absolute = key_index - margin + device_index * atom_count
    usable = (absolute >= 0) & (absolute < atom_count * devices)
    query_heads = queries.reshape(blocks, QBLOCK, HEADS, head_dim)
    key_heads = windows[:, :, :atom_width].reshape(blocks, KWIN, HEADS, head_dim)
    value_heads = windows[:, :, atom_width:].reshape(blocks, KWIN, HEADS, head_dim)
    scores = (
        jnp.einsum("bqhd,bkhd->bhqk", query_heads, key_heads, preferred_element_type=jnp.float32)
        / math.sqrt(head_dim)
        + attn_bias
    )
    scores = jnp.where(usable[:, None, None, :], scores, -1e30)
    shifted = jnp.exp(scores - jnp.max(scores, axis=-1, keepdims=True))
    weights = (shifted / jnp.sum(shifted, axis=-1, keepdims=True)).astype(jnp.bfloat16)
    attended = jnp.einsum(
        "bhqk,bkhd->bqhd", weights, value_heads, preferred_element_type=jnp.float32
    ).reshape(atom_count, atom_width)
    gated = (attended * gating).astype(jnp.bfloat16)
    updated = atoms.astype(jnp.float32) + jnp.dot(
        gated, w_attn_out, preferred_element_type=jnp.float32
    )
    hidden = jax.nn.relu(
        jnp.dot(updated.astype(jnp.bfloat16), w_single, preferred_element_type=jnp.float32)
    ).astype(jnp.bfloat16)
    bounds = jnp.cumsum(token_atoms)
    positions = device_index * atom_count + jnp.arange(atom_count, dtype=jnp.int32)
    owners = jnp.sum((bounds[None, :] <= positions[:, None]).astype(jnp.int32), axis=1)
    one_hot = (owners[:, None] == jnp.arange(tokens, dtype=jnp.int32)[None, :]).astype(jnp.bfloat16)
    token_share = tokens // devices
    summed = lax.psum_scatter(
        lax.dot_general(
            one_hot, hidden, (((0,), (0,)), ((), ())), preferred_element_type=jnp.float32
        ),
        ("row", "col"),
        scatter_dimension=0,
        tiled=True,
    )
    counts = lax.dynamic_slice_in_dim(
        token_atoms, device_index * token_share, token_share, 0
    ).astype(jnp.float32)
    single = (summed / counts[:, None]).astype(jnp.bfloat16)
    left_proj = jnp.dot(single, w_pair_left, preferred_element_type=jnp.float32).astype(
        jnp.bfloat16
    )
    right_proj = jnp.dot(single, w_pair_right, preferred_element_type=jnp.float32).astype(
        jnp.bfloat16
    )
    back_proj = jnp.dot(single, w_atom_back, preferred_element_type=jnp.float32).astype(
        jnp.bfloat16
    )
    left_rows = lax.all_gather(left_proj, "col", axis=0, tiled=True)
    right_all, back_all = (
        lax.all_gather(right_proj, ("row", "col"), axis=0, tiled=True),
        lax.all_gather(back_proj, ("row", "col"), axis=0, tiled=True),
    )
    atoms_out = (updated + jnp.dot(one_hot, back_all, preferred_element_type=jnp.float32)).astype(
        jnp.bfloat16
    )
    right_cols = lax.dynamic_slice_in_dim(
        right_all, lax.axis_index("col") * tile_cols, tile_cols, 0
    )
    merged = (
        pair.astype(jnp.float32)
        + left_rows.T.astype(jnp.float32)[:, :, None]
        + right_cols.T.astype(jnp.float32)[:, None, :]
    )
    pair_norm = layer_norm(merged, 0).astype(jnp.bfloat16)
    inputs_left = jnp.einsum(
        "cij,cd->dij", pair_norm, w_tri_in[:, : 2 * channels], preferred_element_type=jnp.float32
    )
    factor_left = (inputs_left[:channels] * jax.nn.sigmoid(inputs_left[channels:])).astype(
        jnp.bfloat16
    )
    inputs_right = jnp.einsum(
        "cij,cd->dij", pair_norm, w_tri_in[:, 2 * channels :], preferred_element_type=jnp.float32
    )
    factor_right = (inputs_right[:channels] * jax.nn.sigmoid(inputs_right[channels:])).astype(
        jnp.bfloat16
    )
    got_left, got_right = (
        lax.all_to_all(
            factor_left.reshape(channels, 1, tile_rows, tile_cols),
            ("row", "col"),
            split_axis=0,
            concat_axis=1,
            tiled=True,
        ),
        lax.all_to_all(
            factor_right.reshape(channels, 1, tile_rows, tile_cols),
            ("row", "col"),
            split_axis=0,
            concat_axis=1,
            tiled=True,
        ),
    )
    full_left = (
        got_left.reshape(per_channel, row_devices, col_devices, tile_rows, tile_cols)
        .transpose(0, 1, 3, 2, 4)
        .reshape(per_channel, tokens, tokens)
    )
    full_right = (
        got_right.reshape(per_channel, row_devices, col_devices, tile_rows, tile_cols)
        .transpose(0, 1, 3, 2, 4)
        .reshape(per_channel, tokens, tokens)
    )
    triangle = jnp.einsum(
        "eik,ejk->eij", full_left, full_right, preferred_element_type=jnp.float32
    ).astype(jnp.bfloat16)
    blocked = (
        triangle.reshape(per_channel, row_devices, tile_rows, col_devices, tile_cols)
        .transpose(0, 1, 3, 2, 4)
        .reshape(per_channel, devices, tile_rows, tile_cols)
    )
    returned = lax.all_to_all(
        blocked, ("row", "col"), split_axis=1, concat_axis=0, tiled=True
    ).reshape(channels, tile_rows, tile_cols)
    tri_norm = layer_norm(returned.astype(jnp.float32), 0).astype(jnp.bfloat16)
    update = jnp.einsum("cij,cd->dij", tri_norm, w_tri_out, preferred_element_type=jnp.float32)
    gate_pair = jax.nn.sigmoid(
        jnp.einsum("cij,cd->dij", pair_norm, w_tri_gate, preferred_element_type=jnp.float32)
    )
    pair_out = (merged + gate_pair * update).astype(jnp.bfloat16)
    return (atoms_out, pair_out)


def solution(mesh):
    in_specs = (
        P(("row", "col"), None),
        P(None, "row", "col"),
        P(),
        P(("row", "col"), None, None, None),
        P(),
        P(),
        P(),
        P(),
        P(),
        P(),
        P(),
        P(),
        P(),
    )
    out_specs = (P(("row", "col"), None), P(None, "row", "col"))
    return jax.shard_map(
        on_device, mesh=mesh, in_specs=in_specs, out_specs=out_specs, check_vma=False
    )
```

profile of v0, /device:TPU:1, one launch (start us, length us, event | category | flops | bytes accessed | tf_op | source)
XLA Modules:
  0.0 890.7 jit_solution(13415095487594615374)
XLA Ops:
  32.5 12.7 %copy.51 = bf16[128,256,128]{0,2,1:T(8,128)(2,1)} copy(bf16[128,256,128]{2,1,0:T(8,128)(2,1)} %param.14) | data formatting | bytes 16777216 | tf_op args[1]
  45.9 195.2 %reduce-scatter.2.cloned.1.call-done = f32[16,384]{1,0:T(8,128)} async-done(((f32[2048,384]{1,0:T(8,128)}), f32[16,384]{1,0:T(8,128)}) %reduce-scatter.2.cloned.1.call-update) | async-done | bytes 24592 | tf_op jit(solution)/shard_map/reduce_scatter | solution.py:104
  242.1 52.4 %all_gather.11 = bf16[2048,128]{1,0:T(8,128)(2,1)S(1)} all-gather(bf16[16,128]{1,0:T(8,128)(2,1)S(1)} %convolution_convert_fusion), channel_id=1, replica_groups=mesh['row'=8,'col'=16] {'row','col'}, dimensions={0}, use_global_device_ids=true | all-gather | bytes 528384 | tf_op jit(solution)/shard_map/all_gather | solution.py:127
  295.4 16.9 %all_gather.10 = bf16[256,128]{1,0:T(8,128)(2,1)S(1)} all-gather(bf16[16,128]{1,0:T(8,128)(2,1)S(1)} %convolution_convert_fusion.1), channel_id=1, replica_groups=mesh['row'=8,'col'=16] {'col'}, dimensions={0}, use_global_device_ids=true | all-gather | bytes 69632 | tf_op jit(solution)/shard_map/all_gather | solution.py:125
  320.2 10.9 %multiply_reduce_fusion = f32[256,128]{1,0:T(8,128)S(1)} fusion(bf16[128,256,128]{0,2,1:T(8,128)(2,1)} %copy.51, f32[256,128]{1,0:T(8,128)S(1)} %broadcast_multiply_fusion.1, f32[128,128]{0,1:T(8,128)S(1)} %convert_bitcast_fusion.3, f32[128,256]{0,1:T(8,128)S(1)} %convert_bitcast_fusion.2), kind=kLoop, calls=%fused_computation.22 | loop fusion | flops 25133056 | bytes 8847360 | tf_op jit(solution)/shard_map/reduce_sum | solution.py:32
  331.1 14.7 %convolution_bitcast_fusion.1 = f32[256,256,128]{0,2,1:T(8,128)} fusion(bf16[128,512]{1,0:T(8,128)(2,1)S(1)} %copy-done.2, bf16[128,256,128]{0,2,1:T(8,128)(2,1)} %copy.51, f32[256,128]{1,0:T(8,128)S(1)} %add_rsqrt_fusion.1, f32[256,128]{1,0:T(8,128)S(1)} %broadcast_multiply_fusion.1, f32[128,128]{0,1:T(8,128)S(1)} %convert_bitcast_fusion.3, ...), kind=kOutput, calls=%fused_computation.29 | convolution fusion | flops 2172649472 | bytes 42467328 | tf_op jit(solution)/shard_map/cij,cd->dij/dot_general | solution.py:142
  345.8 14.9 %fusion.26 = bf16[128,1,256,128]{0,3,2,1:T(8,128)(2,1)} fusion(f32[256,256,128]{0,2,1:T(8,128)} %convolution_bitcast_fusion.1), kind=kLoop, calls=%fused_computation.38 | loop fusion | flops 20971520 | bytes 41943040 | tf_op jit(solution)/shard_map/reshape | solution.py:156
  360.7 12.2 %copy.52 = bf16[128,1,256,128]{3,2,1,0:T(8,128)(2,1)} copy(bf16[128,1,256,128]{0,3,2,1:T(8,128)(2,1)} %fusion.26) | data formatting | bytes 16777216 | tf_op jit(solution)/shard_map/reshape | solution.py:156
  372.9 10.2 %all-to-all-start = ((bf16[128,1,256,128]{3,2,1,0:T(8,128)(2,1)}), bf16[128,1,256,128]{3,2,1,0:T(8,128)(2,1)}, u32[]{:S(2)}, u32[]{:S(2)}) async-start(bf16[128,1,256,128]{3,2,1,0:T(8,128)(2,1)} %copy.52), calls=%async_computation.1 | async-start | bytes 16777216 | tf_op jit(solution)/shard_map/all_to_all | solution.py:155
  383.0 14.7 %convolution_bitcast_fusion = f32[256,256,128]{0,2,1:T(8,128)} fusion(bf16[128,512]{1,0:T(8,128)(2,1)S(1)} %copy-done.2, bf16[128,256,128]{0,2,1:T(8,128)(2,1)} %copy.51, f32[256,128]{1,0:T(8,128)S(1)} %add_rsqrt_fusion.1, f32[256,128]{1,0:T(8,128)S(1)} %broadcast_multiply_fusion.1, f32[128,128]{0,1:T(8,128)S(1)} %convert_bitcast_fusion.3, ...), kind=kOutput, calls=%fused_computation.28 | convolution fusion | flops 2172649472 | bytes 42467328 | tf_op jit(solution)/shard_map/cij,cd->dij/dot_general | solution.py:148
  397.7 14.9 %fusion.25 = bf16[128,1,256,128]{0,3,2,1:T(8,128)(2,1)} fusion(f32[256,256,128]{0,2,1:T(8,128)} %convolution_bitcast_fusion), kind=kLoop, calls=%fused_computation.37 | loop fusion | flops 20971520 | bytes 41943040 | tf_op jit(solution)/shard_map/reshape | solution.py:163
  412.6 11.8 %copy.54 = bf16[128,1,256,128]{3,2,1,0:T(8,128)(2,1)} copy(bf16[128,1,256,128]{0,3,2,1:T(8,128)(2,1)} %fusion.25) | data formatting | bytes 16777216 | tf_op jit(solution)/shard_map/reshape | solution.py:163
  424.4 60.0 %all-to-all-done = bf16[128,1,256,128]{3,2,1,0:T(8,128)(2,1)} async-done(((bf16[128,1,256,128]{3,2,1,0:T(8,128)(2,1)}), bf16[128,1,256,128]{3,2,1,0:T(8,128)(2,1)}, u32[]{:S(2)}, u32[]{:S(2)}) %all-to-all-start) | async-done | bytes 8388640 | tf_op jit(solution)/shard_map/all_to_all | solution.py:155
  484.4 10.4 %all-to-all-start.1 = ((bf16[128,1,256,128]{3,2,1,0:T(8,128)(2,1)}), bf16[128,1,256,128]{3,2,1,0:T(8,128)(2,1)}, u32[]{:S(2)}, u32[]{:S(2)}) async-start(bf16[128,1,256,128]{3,2,1,0:T(8,128)(2,1)} %copy.54), calls=%async_computation.2 | async-start | bytes 16777216 | tf_op jit(solution)/shard_map/all_to_all | solution.py:162
  494.8 12.0 %copy.53 = bf16[1,8,256,16,128]{4,3,2,1,0:T(8,128)(2,1)} copy(bf16[1,8,256,16,128]{4,2,3,1,0:T(8,128)(2,1)} %bitcast.14) | data formatting | bytes 16777216 | tf_op jit(solution)/shard_map/transpose | solution.py:172
  506.8 88.1 %all-to-all-done.1 = bf16[128,1,256,128]{3,2,1,0:T(8,128)(2,1)} async-done(((bf16[128,1,256,128]{3,2,1,0:T(8,128)(2,1)}), bf16[128,1,256,128]{3,2,1,0:T(8,128)(2,1)}, u32[]{:S(2)}, u32[]{:S(2)}) %all-to-all-start.1) | async-done | bytes 8388640 | tf_op jit(solution)/shard_map/all_to_all | solution.py:162
  594.9 12.0 %copy.55 = bf16[1,8,256,16,128]{4,3,2,1,0:T(8,128)(2,1)} copy(bf16[1,8,256,16,128]{4,2,3,1,0:T(8,128)(2,1)} %bitcast.19) | data formatting | bytes 16777216 | tf_op jit(solution)/shard_map/transpose | solution.py:177
  606.9 24.3 %convert_bitcast_fusion.1 = bf16[256,8,16,128]{3,1,2,0:T(8,128)(2,1)} fusion(bf16[256,8,16,128]{3,2,1,0:T(8,128)(2,1)} %bitcast.93, bf16[256,8,16,128]{3,2,1,0:T(8,128)(2,1)} %bitcast.92), kind=kOutput, calls=%fused_computation.36 | convolution fusion | flops 17184063488 | bytes 25165824 | tf_op jit(solution)/shard_map/eik,ejk->eij/dot_general | solution.py:180
  649.9 10.7 %all-to-all-start.2 = ((bf16[1,128,256,128]{3,2,0,1:T(8,128)(2,1)}), bf16[1,128,256,128]{3,2,0,1:T(8,128)(2,1)}, u32[]{:S(2)}, u32[]{:S(2)}) async-start(bf16[1,128,256,128]{3,2,0,1:T(8,128)(2,1)} %bitcast.90), calls=%async_computation.3 | async-start | bytes 16777216 | tf_op jit(solution)/shard_map/all_to_all | solution.py:188
  660.9 146.4 %all_gather.9 = bf16[2048,128]{1,0:T(8,128)(2,1)S(1)} all-gather(bf16[16,128]{1,0:T(8,128)(2,1)S(1)} %convolution_convert_fusion.2), channel_id=1, replica_groups=mesh['row'=8,'col'=16] {'row','col'}, dimensions={0}, use_global_device_ids=true | all-gather | bytes 528384 | tf_op jit(solution)/shard_map/all_gather | solution.py:128
  808.3 15.3 %fusion.60 = f32[256,128,128]{2,1,0:T(8,128)} fusion(bf16[128,128]{1,0:T(8,128)(2,1)S(1)} %copy-done.3, bf16[128,256,128]{0,2,1:T(8,128)(2,1)} %copy.51, f32[256,128]{1,0:T(8,128)S(1)} %add_rsqrt_fusion.1, f32[256,128]{1,0:T(8,128)S(1)} %broadcast_multiply_fusion.1, f32[128,128]{0,1:T(8,128)S(1)} %convert_bitcast_fusion.3, ...), kind=kOutput, calls=%fused_computation.87 | convolution fusion | flops 1098907648 | bytes 25657344 | tf_op jit(solution)/shard_map/cij,cd->dij/dot_general | solution.py:194
  833.8 10.3 %fusion.5 = bf16[128,256,128]{2,1,0:T(8,128)(2,1)} fusion(bf16[1,128,256,128]{3,2,0,1:T(8,128)(2,1)} %all-to-all-done.2, f32[256,128]{1,0:T(8,128)S(1)} %add_rsqrt_fusion, f32[256,128]{1,0:T(8,128)S(1)} %broadcast_multiply_fusion), kind=kLoop, calls=%fused_computation.8 | loop fusion | flops 16777216 | bytes 17039360 | tf_op jit(solution)/shard_map/convert_element_type | solution.py:191
  844.1 27.1 %fusion.14 = bf16[128,256,128]{0,2,1:T(8,128)(2,1)} fusion(f32[256,128,128]{2,1,0:T(8,128)} %fusion.60, bf16[128,256,128]{0,2,1:T(8,128)(2,1)} %copy.51, bf16[128,256,128]{2,1,0:T(8,128)(2,1)} %fusion.5, f32[128,128]{0,1:T(8,128)S(1)} %convert_bitcast_fusion.3, f32[128,256]{0,1:T(8,128)S(1)} %convert_bitcast_fusion.2, bf16[128,128]{1,0:T(8,128)(2,1)S(1)} %copy-done.7), kind=kOutput, calls=%fused_computation.20 | convolution fusion | flops 1111490560 | bytes 42172416 | tf_op jit(solution)/shard_map/cij,cd->dij/dot_general | solution.py:192
  871.2 12.4 %copy.59 = bf16[128,256,128]{2,1,0:T(8,128)(2,1)} copy(bf16[128,256,128]{0,2,1:T(8,128)(2,1)} %fusion.14) | data formatting | bytes 16777216
  (73 shorter events, 65.6 us)
Async XLA Ops:
  7.2 2.0 copy-start
  7.2 234.0 %copy-start.4 = (bf16[384,128]{1,0:T(8,128)(2,1)S(1)}, bf16[384,128]{1,0:T(8,128)(2,1)}, u32[]{:S(2)}) copy-start(bf16[384,128]{1,0:T(8,128)(2,1)} %param.21) | copy-start | bytes 294916
  7.2 287.3 %copy-start.5 = (bf16[384,128]{1,0:T(8,128)(2,1)S(1)}, bf16[384,128]{1,0:T(8,128)(2,1)}, u32[]{:S(2)}) copy-start(bf16[384,128]{1,0:T(8,128)(2,1)} %param.20) | copy-start | bytes 294916
  7.2 233.9 %reduce-scatter.2.cloned.1.call-start = ((), (), s32[]{:S(2)}) async-start(), calls=%async_computation.4 | async-start | bytes 3170304 | tf_op jit(solution)/shard_map/reduce_scatter | solution.py:104
  10.2 13.1 %collective-permute-start = (bf16[48,256]{1,0:T(8,128)(2,1)S(1)}, bf16[48,256]{1,0:T(8,128)(2,1)S(1)}, u32[]{:S(2)}, u32[]{:S(2)}) collective-permute-start(bf16[48,256]{1,0:T(8,128)(2,1)S(1)} %get-tuple-element.12), channel_id=1, source_target_pairs={{0,1},{1,2},{2,3},{3,4},{4,5},{5,6},{6,7},{7,8},{8,9},{9,10},{10,1... | collective-permute-start | bytes 73736 | tf_op jit(solution)/shard_map/ppermute | solution.py:23
  14.6 8.7 collective-permute-start.1
  32.4 298.7 %copy-start.2 = (bf16[128,512]{1,0:T(8,128)(2,1)S(1)}, bf16[128,512]{1,0:T(8,128)(2,1)}, u32[]{:S(2)}) copy-start(bf16[128,512]{1,0:T(8,128)(2,1)} %param.23) | copy-start | bytes 393220
  372.9 111.5 %all-to-all-start = ((bf16[128,1,256,128]{3,2,1,0:T(8,128)(2,1)}), bf16[128,1,256,128]{3,2,1,0:T(8,128)(2,1)}, u32[]{:S(2)}, u32[]{:S(2)}) async-start(bf16[128,1,256,128]{3,2,1,0:T(8,128)(2,1)} %copy.52), calls=%async_computation.1 | async-start | bytes 16777216 | tf_op jit(solution)/shard_map/all_to_all | solution.py:155
  484.4 110.5 %all-to-all-start.1 = ((bf16[128,1,256,128]{3,2,1,0:T(8,128)(2,1)}), bf16[128,1,256,128]{3,2,1,0:T(8,128)(2,1)}, u32[]{:S(2)}, u32[]{:S(2)}) async-start(bf16[128,1,256,128]{3,2,1,0:T(8,128)(2,1)} %copy.54), calls=%async_computation.2 | async-start | bytes 16777216 | tf_op jit(solution)/shard_map/all_to_all | solution.py:162
  641.0 19.7 %copy-start.6 = (bf16[384,128]{1,0:T(8,128)(2,1)S(1)}, bf16[384,128]{1,0:T(8,128)(2,1)}, u32[]{:S(2)}) copy-start(bf16[384,128]{1,0:T(8,128)(2,1)} %param.22) | copy-start | bytes 294916
  641.0 19.7 %copy-start.8 = (f32[16,384]{1,0:T(8,128)S(1)}, f32[16,384]{1,0:T(8,128)}, u32[]{:S(2)}) copy-start(f32[16,384]{1,0:T(8,128)} %reduce-scatter.2.cloned.1.call-done) | copy-start | bytes 73732
  641.0 167.3 %copy-start.3 = (bf16[128,128]{1,0:T(8,128)(2,1)S(1)}, bf16[128,128]{1,0:T(8,128)(2,1)}, u32[]{:S(2)}) copy-start(bf16[128,128]{1,0:T(8,128)(2,1)} %param.24) | copy-start | bytes 98308
  649.9 173.7 %all-to-all-start.2 = ((bf16[1,128,256,128]{3,2,0,1:T(8,128)(2,1)}), bf16[1,128,256,128]{3,2,0,1:T(8,128)(2,1)}, u32[]{:S(2)}, u32[]{:S(2)}) async-start(bf16[1,128,256,128]{3,2,0,1:T(8,128)(2,1)} %bitcast.90), calls=%async_computation.3 | async-start | bytes 16777216 | tf_op jit(solution)/shard_map/all_to_all | solution.py:188
  823.6 20.5 %copy-start.7 = (bf16[128,128]{1,0:T(8,128)(2,1)S(1)}, bf16[128,128]{1,0:T(8,128)(2,1)}, u32[]{:S(2)}) copy-start(bf16[128,128]{1,0:T(8,128)(2,1)} %param.25) | copy-start | bytes 98308
  844.1 39.5 %copy-start.1 = (bf16[128,512]{1,0:T(8,128)(2,1)S(1)}, bf16[128,512]{1,0:T(8,128)(2,1)}, u32[]{:S(2)}) copy-start(bf16[128,512]{1,0:T(8,128)(2,1)} %param.17) | copy-start | bytes 393220
Sparse Core Ops, SparseCore 0:
  32.6 208.5 reduce-scatter.1
where the time goes:
time: 897 us; the launch traced here: 891 us
  waiting for transfers between devices  343 us (38%)
  blocking collectives  216 us (24%)
  matrix products  106 us (12%)
  local copies, waits for them, and re-layouts  94.7 us (11%)
  other arithmetic  73.5 us (8%)
  starting transfers between devices  42.5 us (5%)
  between operations  14.6 us (2%)
    reduce_scatter x1, waiting for transfers between devices, on_device(): lax.psum_scatter(lax.dot_general(one_hot, hidden, (((0,), (0,)), ((), ())...  195 us
    all_gather x1, blocking collectives, on_device(): lax.all_gather(back_proj, ('row', 'col'), axis=0, tiled=True)  146 us
    all_to_all x1, waiting for transfers between devices, on_device(): lax.all_to_all(factor_right.reshape(channels, 1, tile_rows, tile_cols), (...  88.1 us
    all_to_all x1, waiting for transfers between devices, on_device(): lax.all_to_all(factor_left.reshape(channels, 1, tile_rows, tile_cols), ('...  60 us
    all_gather x1, blocking collectives, on_device(): lax.all_gather(right_proj, ('row', 'col'), axis=0, tiled=True)  52.4 us
    unnamed x23, local copies, waits for them, and re-layouts  35.2 us
    dot_general x1, matrix products, on_device(): jnp.einsum('cij,cd->dij', tri_norm, w_tri_out, preferred_element_type=jnp...  27.1 us
    dot_general x1, matrix products, on_device(): jnp.einsum('eik,ejk->eij', full_left, full_right, preferred_element_type=...  24.3 us
  transfers between devices with their start and end apart: 6, of which 3 were waited for; matrix products, arithmetic and copies ran while one was open for 10% of the time, Pallas kernels for 0%

commit v1 on v0

v1 whole, which is shorter than its diff:
```python
import functools
import math

import jax
import jax.numpy as jnp
from jax import lax
from jax.experimental import pallas as pl
from jax.experimental.pallas import tpu as pltpu
from jax.sharding import PartitionSpec as P

HEADS = 4
QBLOCK = 32
KWIN = 128
EPSILON = 1e-05
MESH_AXES = ("row", "col")

ROWS_PER_STEP = 32
GROUP = 16
CHUNK = 8
FINISH_CHUNK = 4
FIRST, SECOND = (0, 4), (4, 8)
RIGHT_FIRST, RIGHT_SECOND = (0, 5), (5, 8)
SINGLES = 1280
SLOTS = 8
VMEM_BYTES = 63_000_000
ATOM_VMEM_BYTES = 63_400_000
FRONT_VMEM_BYTES = 62_000_000
TOKEN_VMEM_BYTES = 40_000_000

f32 = jnp.float32
bf16 = jnp.bfloat16


def kernel_params(limit=VMEM_BYTES):
    return pltpu.CompilerParams(vmem_limit_bytes=limit)


def vmem():
    return pl.BlockSpec(memory_space=pltpu.VMEM)


def whole(array):
    return pl.BlockSpec(array.shape, lambda i: (0,) * len(array.shape))


def sigmoid(x):
    return 0.5 * jnp.tanh(0.5 * x) + 0.5


def normalise(values, along):
    average = jnp.mean(values, axis=along, keepdims=True)
    centred = values - average
    variance = jnp.mean(centred * centred, axis=along, keepdims=True)
    return centred * lax.rsqrt(variance + EPSILON)


def dot(a, b, contract_a, contract_b):
    return lax.dot_general(
        a, b, (((contract_a,), (contract_b,)), ((), ())), preferred_element_type=f32
    )


def atom_kernel(
    total_atoms,
    first_ref,
    before_ref,
    after_ref,
    counts_ref,
    *refs,
):
    fetched = refs[:8]
    atoms_out_ref, partial_ref = refs[8:10]
    held, sems = refs[10:18], refs[18]
    copies = [
        pltpu.make_async_copy(source, target, sems.at[k])
        for k, (source, target) in enumerate(zip(fetched, held))
    ]
    for copy in copies:
        copy.start()
    atoms_ref, w_attn_ref, bias_ref, w_attn_out_ref = held[:4]
    w_single_ref, w_back_ref, w_left_ref, w_right_ref = held[4:]
    first = first_ref[0]
    atom_count, width = atoms_ref.shape
    margin = (KWIN - QBLOCK) // 2
    head_dim = width // HEADS
    reach = margin + QBLOCK
    wide = atom_count + 2 * QBLOCK

    counts = counts_ref[...].astype(f32)
    lane_from = lax.broadcasted_iota(jnp.int32, (width, width), 0)
    lane_to = lax.broadcasted_iota(jnp.int32, (width, width), 1)
    earlier = jnp.where(lane_from <= lane_to, 1.0, 0.0).astype(bf16)
    within = dot(counts.astype(bf16), earlier, 1, 0)
    totals = jnp.broadcast_to(within[:, width - 1 :], within.shape)
    so_far = jnp.zeros((1, width), f32)
    ends, begins = [], []
    for row in range(counts.shape[0]):
        row_ends = within[row : row + 1] + so_far
        ends.append(row_ends)
        begins.append(row_ends - counts[row : row + 1])
        so_far = so_far + totals[row : row + 1]
    ends = jnp.concatenate(ends, axis=1).astype(jnp.int32)
    starts = jnp.concatenate(begins, axis=1).astype(jnp.int32)
    tokens = ends.shape[1]
    position = (first - QBLOCK) + lax.broadcasted_iota(jnp.int32, (wide, 1), 0)
    member = jnp.where((starts <= position) & (position < ends), 1.0, 0.0).astype(bf16)
    own_member = member[QBLOCK : QBLOCK + atom_count]
    own_position = position[QBLOCK : QBLOCK + atom_count]
    column = lax.broadcasted_iota(jnp.int32, (1, partial_ref.shape[0] * SLOTS), 1)
    wanted = jnp.where(
        column * 0 + first >= total_atoms - SINGLES,
        first + (column >> (SLOTS.bit_length() - 1)),
        jnp.where(column < tokens - SINGLES, starts[:, : column.shape[1]], -1),
    )
    chosen = jnp.where(wanted == own_position, 1.0, 0.0).astype(bf16)
    together = dot(own_member, member, 1, 1).astype(bf16)
    own_count = jnp.sum(together.astype(f32), axis=1, keepdims=True)

    copies[0].wait()
    atoms = jnp.concatenate(
        [before_ref[:reach], atoms_ref[...].astype(f32), after_ref[:reach]], axis=0
    )
    normed = normalise(atoms, 1).astype(bf16)
    copies[1].wait()
    projected = dot(normed, w_attn_ref[...], 1, 0)
    kv = projected[:, width : 3 * width].astype(bf16)
    queries = projected[margin : margin + wide, :width]
    gating = sigmoid(projected[margin : margin + wide, 3 * width :])
    feature = lax.broadcasted_iota(jnp.int32, (QBLOCK, width), 1)
    in_head = [
        (feature >= head * head_dim) & (feature < (head + 1) * head_dim) for head in range(HEADS)
    ]
    window_at = lax.broadcasted_iota(jnp.int32, (HEADS * QBLOCK, KWIN), 1)
    copies[2].wait()
    attended = []
    blocks = wide // QBLOCK
    for block in range(blocks):
        start = block * QBLOCK
        query = queries[start : start + QBLOCK]
        query_heads = jnp.concatenate(
            [jnp.where(mask, query, 0.0) for mask in in_head], axis=0
        ).astype(bf16)
        keys = kv[start : start + KWIN, :width]
        values = kv[start : start + KWIN, width:]
        if block == 0:
            bias = before_ref[reach:]
        elif block == blocks - 1:
            bias = after_ref[reach:]
        else:
            bias = bias_ref[block - 1]
        scores = dot(query_heads, keys, 1, 1) / math.sqrt(head_dim) + bias
        absolute = window_at + (first + start - reach)
        scores = jnp.where((absolute >= 0) & (absolute < total_atoms), scores, -1e30)
        shifted = jnp.exp(scores - jnp.max(scores, axis=1, keepdims=True))
        weights = (shifted / jnp.sum(shifted, axis=1, keepdims=True)).astype(bf16)
        heads_out = dot(weights, values, 1, 0)
        joined = jnp.zeros((QBLOCK, width), f32)
        for head, mask in enumerate(in_head):
            joined = jnp.where(mask, heads_out[head * QBLOCK : (head + 1) * QBLOCK], joined)
        attended.append(joined)
    gated = (jnp.concatenate(attended, axis=0) * gating).astype(bf16)
    for copy in copies[3:]:
        copy.wait()
    updated = atoms[margin : margin + wide] + dot(gated, w_attn_out_ref[...], 1, 0)
    hidden = jnp.maximum(dot(updated.astype(bf16), w_single_ref[...], 1, 0), 0.0).astype(bf16)
    single = (dot(together, hidden, 1, 0) / own_count).astype(bf16)
    back = dot(single, w_back_ref[...], 1, 0).astype(bf16).astype(f32)
    atoms_out_ref[...] = (updated[QBLOCK : QBLOCK + atom_count] + back).astype(bf16)

    sides = [dot(single, ref[...], 1, 0).astype(bf16) for ref in (w_left_ref, w_right_ref)]
    shape = (partial_ref.shape[0], SLOTS, width)
    partial_ref[...] = jnp.concatenate(
        [dot(chosen, side, 0, 0).reshape(shape) for side in sides], axis=1
    ).astype(bf16)


def spread_kernel(rows, cols, got_ref, out_ref):
    got = got_ref[...].astype(f32)
    devices = rows * cols
    width = got.shape[2]
    first_single = devices - SINGLES // width
    summed = jnp.sum(got[:first_single], axis=0)
    slot = lax.broadcasted_iota(jnp.int32, (SLOTS, width), 0)
    lefts, rights = [], []
    for row in range(rows):
        at = 2 * row - (2 * rows - SINGLES // width)
        if at < 0:
            lefts.append(summed[:SLOTS])
        else:
            at += first_single
            lefts.append(jnp.where(slot == 0, got[at, :SLOTS], got[at + 1, :SLOTS]))
    for col in range(cols):
        at = col - (cols - SINGLES // width)
        rights.append(summed[SLOTS:] if at < 0 else got[first_single + at, SLOTS:])
    for row in range(rows):
        for col in range(cols):
            block = jnp.concatenate([lefts[row], rights[col]], axis=0)
            out_ref[row * cols + col] = block.astype(bf16)


def gather_kernel(rows, cols, place_ref, got_ref, out_ref, held_ref):
    row, col = place_ref[0], place_ref[1]
    devices, slots, width = got_ref.shape
    held_ref[...] = got_ref[...].astype(f32).reshape(devices * slots, width)
    single_rows = rows - SINGLES // width // 2
    single_cols = cols - SINGLES // width
    owners = width // SLOTS

    @pl.when(row < single_rows)
    def _():
        blocks = held_ref[pl.ds(row * (2 * owners * slots), 2 * owners * slots), :]
        out_ref[: 2 * width] = blocks.reshape(2 * owners, slots, width)[:, :SLOTS].reshape(
            2 * width, width
        )

    @pl.when(row >= single_rows)
    def _():
        out_ref[:width] = held_ref[pl.ds(0, width, stride=slots), :]
        out_ref[width : 2 * width] = held_ref[pl.ds(1, width, stride=slots), :]

    @pl.when(col < single_cols)
    def _():
        blocks = held_ref[pl.ds(col * (owners * slots), owners * slots), :]
        right = blocks.reshape(owners, slots, width)[:, SLOTS:].reshape(width, width)
        out_ref[2 * width :] = right.T

    @pl.when(col >= single_cols)
    def _():
        out_ref[2 * width :] = held_ref[pl.ds(SLOTS, width, stride=slots), :].T


def exchange(blocks):
    return lax.all_to_all(blocks, MESH_AXES, split_axis=0, concat_axis=0, tiled=True)


def atom_stage(
    pair,
    atoms,
    token_atoms,
    attn_bias,
    w_attn,
    w_attn_out,
    w_single,
    w_pair_left,
    w_pair_right,
    w_atom_back,
):
    atom_count, width = atoms.shape
    tokens = token_atoms.shape[0]
    rows, cols = lax.axis_size("row"), lax.axis_size("col")
    devices = rows * cols
    reach = (KWIN - QBLOCK) // 2 + QBLOCK
    place = jnp.stack([lax.axis_index("row"), lax.axis_index("col")]).astype(jnp.int32)
    first = (lax.axis_index(MESH_AXES) * atom_count).astype(jnp.int32).reshape(1)
    bias = attn_bias.reshape(atom_count // QBLOCK, HEADS * QBLOCK, KWIN)
    up = [(i, i + 1) for i in range(devices - 1)]
    down = [(j, i) for i, j in up]
    before = lax.ppermute(
        jnp.concatenate([atoms[atom_count - reach :].astype(f32), bias[-1]], axis=0), MESH_AXES, up
    )
    after = lax.ppermute(
        jnp.concatenate([atoms[:reach].astype(f32), bias[0]], axis=0), MESH_AXES, down
    )
    small = (before, after, token_atoms.reshape(tokens // width, width))
    fetched = (
        atoms,
        w_attn,
        bias,
        w_attn_out,
        w_single,
        w_atom_back,
        w_pair_left,
        w_pair_right,
    )
    results = (
        jax.ShapeDtypeStruct((atom_count, width), bf16),
        jax.ShapeDtypeStruct((devices, 2 * SLOTS, width), bf16),
    )
    atoms_out, partial = pl.pallas_call(
        functools.partial(atom_kernel, atom_count * devices),
        out_shape=results,
        grid=(1,),
        in_specs=[pl.BlockSpec(memory_space=pltpu.SMEM)]
        + [whole(x) for x in small]
        + [pl.BlockSpec(memory_space=pltpu.HBM)] * len(fetched),
        out_specs=tuple(whole(x) for x in results),
        scratch_shapes=[pltpu.VMEM(x.shape, x.dtype) for x in fetched]
        + [pltpu.SemaphoreType.DMA((len(fetched),))],
        compiler_params=kernel_params(ATOM_VMEM_BYTES),
        cost_estimate=pl.CostEstimate(
            flops=400_000_000, bytes_accessed=3_000_000, transcendentals=100_000
        ),
        name="atom_attention",
    )(first, *small, *fetched)
    partial, pair = lax.optimization_barrier((partial, pair))
    got = exchange(partial)
    got, lanes = lax.optimization_barrier((got, to_lanes(pair, FIRST, None)))
    spread = pl.pallas_call(
        functools.partial(spread_kernel, rows, cols),
        out_shape=jax.ShapeDtypeStruct(got.shape, bf16),
        in_specs=[vmem()],
        out_specs=vmem(),
        compiler_params=kernel_params(TOKEN_VMEM_BYTES),
        name="spread_tokens",
    )(got)
    spread, pair = lax.optimization_barrier((spread, pair))
    shared = exchange(spread)
    shared, lanes = lax.optimization_barrier((shared, to_lanes(pair, SECOND, lanes)))
    sides = pl.pallas_call(
        functools.partial(gather_kernel, rows, cols),
        out_shape=jax.ShapeDtypeStruct((3 * width, width), f32),
        in_specs=[pl.BlockSpec(memory_space=pltpu.SMEM), vmem()],
        out_specs=vmem(),
        scratch_shapes=[pltpu.VMEM((devices * 2 * SLOTS, width), f32)],
        compiler_params=kernel_params(TOKEN_VMEM_BYTES),
        name="gather_tokens",
    )(place, shared)
    return atoms_out, lanes, sides


def interleave(*weights):
    channels = weights[0].shape[0]
    tiles = jnp.stack([w.reshape(channels // 8, 8, w.shape[1]) for w in weights], axis=1)
    return tiles.reshape(len(weights) * channels, weights[0].shape[1])


def turned_scratch(channels):
    return pltpu.VMEM((ROWS_PER_STEP // GROUP, channels * GROUP, 128), f32)


def lanes_kernel(pair_ref, *rest):
    out_ref, turned_ref = rest[-2:]
    channels = pair_ref.shape[0]
    for group in range(ROWS_PER_STEP // GROUP):
        rows = slice(group * GROUP, (group + 1) * GROUP)
        turned_ref[group] = pair_ref[:, rows, :].astype(f32).reshape(channels * GROUP, 128)
        for i in range(GROUP):
            at = (group * GROUP + i) * 128
            out_ref[:, at : at + 128] = turned_ref[
                group, pl.ds(i, channels, stride=GROUP), :
            ].astype(bf16)


def right_spec(sides):
    width = sides.shape[1]
    return pl.BlockSpec((width, width), lambda i: (sides.shape[0] // width - 1, 0))


def written_into(operands, in_specs, so_far):
    if so_far is None:
        return operands, in_specs, {}
    spec = pl.BlockSpec(memory_space=pltpu.HBM)
    return operands + (so_far,), in_specs + [spec], {len(operands): 0}


def to_lanes(pair, part, so_far):
    channels, tile_rows, _ = pair.shape
    first, steps = part[0], part[1] - part[0]
    step_lanes = ROWS_PER_STEP * 128
    operands, in_specs, aliases = written_into(
        (pair,),
        [pl.BlockSpec((channels, ROWS_PER_STEP, 128), lambda i: (0, first + i, 0))],
        so_far,
    )
    return pl.pallas_call(
        lanes_kernel,
        grid=(steps,),
        out_shape=jax.ShapeDtypeStruct((channels, tile_rows * 128), bf16),
        in_specs=in_specs,
        out_specs=pl.BlockSpec((channels, step_lanes), lambda i: (0, first + i)),
        input_output_aliases=aliases,
        scratch_shapes=[turned_scratch(channels)],
        compiler_params=kernel_params(),
        cost_estimate=pl.CostEstimate(
            flops=0, bytes_accessed=4 * channels * steps * step_lanes, transcendentals=0
        ),
        name=f"pair_lanes_{first}",
    )(*operands)


def projections_of(left, right, row, chunk):
    return jnp.concatenate(
        [jnp.broadcast_to(left[:, row + i : row + i + 1], right.shape) + right for i in range(chunk)],
        axis=1,
    )


def store_turned(turned_ref, group, row, values):
    channels = values.shape[0]
    for i in range(values.shape[1] // 128):
        turned_ref[group, pl.ds(row + i, channels, stride=GROUP), :] = values[
            :, i * 128 : (i + 1) * 128
        ]


def each_chunk(chunk, prepare, use):
    places = []
    for group in range(ROWS_PER_STEP // GROUP):
        for row in range(0, GROUP, chunk):
            start = (group * GROUP + row) * 128
            places.append((group, row, slice(start, start + chunk * 128)))
    ready = prepare(*places[0])
    for n, place in enumerate(places):
        following = prepare(*places[n + 1]) if n + 1 < len(places) else None
        use(*place, ready)
        ready = following


def front_kernel(parts, pair_ref, left_ref, right_ref, w_ref, *rest):
    gate_refs = rest[-2:-1] if parts % 2 else ()
    out_ref, turned_ref = rest[-2 - parts % 2], rest[-1]
    channels = pair_ref.shape[0]
    weights = w_ref[...]
    left = left_ref[...].T

    def prepare(group, row, at):
        merged = pair_ref[:, at].astype(f32) + projections_of(
            left, right_ref[...], group * GROUP + row, CHUNK
        )
        return dot(weights, normalise(merged, 0).astype(bf16), 1, 0)

    def use(group, row, at, inputs):
        inputs = inputs.reshape(channels // 8, parts, 8, CHUNK * 128)
        factor = inputs[:, 0] * jnp.tanh(inputs[:, 1]) + inputs[:, 0]
        store_turned(turned_ref, group, row, factor.reshape(channels, CHUNK * 128))
        if gate_refs:
            gate = 0.5 * jnp.tanh(inputs[:, parts - 1]) + 0.5
            gate_refs[0][:, at] = gate.reshape(channels, CHUNK * 128).astype(bf16)
        if row + CHUNK == GROUP:
            rows = slice(group * GROUP, (group + 1) * GROUP)
            out_ref[:, rows, :] = turned_ref[group].reshape(channels, GROUP, 128).astype(bf16)

    each_chunk(CHUNK, prepare, use)


def front(pair_lanes, sides, weights, part, name, place=0, total=None, so_far=None):
    channels = pair_lanes.shape[0]
    parts = weights.shape[0] // channels
    first, steps = part[0], part[1] - part[0]
    total = total or steps
    step_lanes = ROWS_PER_STEP * 128
    out_shape = [jax.ShapeDtypeStruct((channels, total * ROWS_PER_STEP, 128), bf16)]
    out_specs = [pl.BlockSpec((channels, ROWS_PER_STEP, 128), lambda i: (0, place + i, 0))]
    if parts % 2:
        out_shape.append(jax.ShapeDtypeStruct((channels, steps * step_lanes), bf16))
        out_specs.append(pl.BlockSpec((channels, step_lanes), lambda i: (0, i)))
    elements = channels * steps * step_lanes
    operands, in_specs, aliases = written_into(
        (pair_lanes, sides, sides, weights),
        [
            pl.BlockSpec((channels, step_lanes), lambda i: (0, first + i)),
            pl.BlockSpec((ROWS_PER_STEP, channels), lambda i: (first + i, 0)),
            right_spec(sides),
            pl.BlockSpec(weights.shape, lambda i: (0, 0)),
        ],
        so_far,
    )
    return pl.pallas_call(
        functools.partial(front_kernel, parts),
        grid=(steps,),
        out_shape=out_shape,
        in_specs=in_specs,
        out_specs=out_specs,
        input_output_aliases=aliases,
        scratch_shapes=[turned_scratch(channels)],
        compiler_params=kernel_params(FRONT_VMEM_BYTES),
        cost_estimate=pl.CostEstimate(
            flops=2 * elements * weights.shape[0],
            bytes_accessed=2 * elements * parts,
            transcendentals=elements * (parts - 1),
        ),
        name=name,
    )(*operands)


def triangle_kernel(left_at, right_at, left_ref, *refs):
    right_refs, out_ref = refs[:-1], refs[-1]
    rows, cols = left_ref.shape[:2]
    right = jnp.concatenate(
        [
            jnp.concatenate([ref[q, at] for q in range(cols)], axis=1)
            for ref, at in zip(right_refs, right_at)
        ],
        axis=0,
    )
    left = jnp.concatenate(
        [
            jnp.concatenate([left_ref[r, q, left_at] for q in range(cols)], axis=1)
            for r in range(rows)
        ],
        axis=0,
    )
    product = dot(left, right, 1, 1).astype(bf16)
    part_rows = out_ref.shape[2]
    for r in range(rows):
        block = product[r * part_rows : (r + 1) * part_rows]
        out_ref[r, 0] = block[:, :128]
        out_ref[r, 1] = block[:, 128:]


def triangle(left, left_at, rights, right_at, rows, cols, name):
    devices, held_rows, _ = left.shape
    part_rows = left_at.stop - left_at.start
    tokens = cols * 128
    left_grid = left.reshape(rows, cols, held_rows, 128)
    product = pl.pallas_call(
        functools.partial(triangle_kernel, left_at, right_at),
        grid=(rows,),
        out_shape=jax.ShapeDtypeStruct((rows, cols, part_rows, 128), bf16),
        in_specs=[
            pl.BlockSpec(left_grid.shape, lambda r: (0, 0, 0, 0), pipeline_mode=pl.Buffered(1)),
        ]
        + [pl.BlockSpec((cols,) + right.shape[1:], lambda r: (r, 0, 0)) for right in rights],
        out_specs=pl.BlockSpec((rows, cols // rows, part_rows, 128), lambda r: (0, r, 0, 0)),
        compiler_params=kernel_params(),
        cost_estimate=pl.CostEstimate(
            flops=2 * rows * part_rows * tokens * tokens,
            bytes_accessed=2 * tokens * (2 * rows * part_rows + tokens),
            transcendentals=0,
        ),
        name=name,
    )(left_grid, *rights)
    return product.reshape(devices, part_rows, 128)


def finish_kernel(back_ref, gate_ref, pair_ref, left_ref, right_ref, w_ref, *rest):
    out_ref, turned_ref, change_ref = rest[-3:]
    channels = pair_ref.shape[0]
    weights = w_ref[...]
    left = left_ref[...].T

    def prepare(group, row, at):
        if row == 0:
            turned_ref[group] = (
                back_ref[:, group * GROUP : (group + 1) * GROUP, :]
                .astype(f32)
                .reshape(channels * GROUP, 128)
            )
        products = jnp.concatenate(
            [
                turned_ref[group, pl.ds(row + i, channels, stride=GROUP), :]
                for i in range(FINISH_CHUNK)
            ],
            axis=1,
        )
        return dot(weights, normalise(products, 0).astype(bf16), 1, 0)

    def use(group, row, at, update):
        change = (
            projections_of(left, right_ref[...], group * GROUP + row, FINISH_CHUNK)
            + gate_ref[:, at].astype(f32) * update
        )
        store_turned(change_ref, group, row, change)
        if row + FINISH_CHUNK == GROUP:
            rows = slice(group * GROUP, (group + 1) * GROUP)
            out_ref[:, rows, :] = (
                pair_ref[:, rows, :].astype(f32)
                + change_ref[group].reshape(channels, GROUP, 128)
            ).astype(bf16)

    each_chunk(FINISH_CHUNK, prepare, use)


def finish(back, gate, pair, sides, weights, part, so_far):
    channels, tile_rows, _ = pair.shape
    step_lanes = ROWS_PER_STEP * 128
    first, steps = part[0], part[1] - part[0]
    block = pl.BlockSpec((channels, ROWS_PER_STEP, 128), lambda i: (0, first + i, 0))
    operands, in_specs, aliases = written_into(
        (back, gate, pair, sides, sides, weights),
        [
            pl.BlockSpec((channels, ROWS_PER_STEP, 128), lambda i: (0, i, 0)),
            pl.BlockSpec((channels, step_lanes), lambda i: (0, i)),
            block,
            pl.BlockSpec((ROWS_PER_STEP, channels), lambda i: (first + i, 0)),
            right_spec(sides),
            pl.BlockSpec(weights.shape, lambda i: (0, 0)),
        ],
        so_far,
    )
    return pl.pallas_call(
        finish_kernel,
        grid=(steps,),
        out_shape=jax.ShapeDtypeStruct(pair.shape, bf16),
        in_specs=in_specs,
        out_specs=block,
        input_output_aliases=aliases,
        scratch_shapes=[turned_scratch(channels)] * 2,
        compiler_params=kernel_params(),
        cost_estimate=pl.CostEstimate(
            flops=2 * back.size * channels, bytes_accessed=8 * back.size, transcendentals=0
        ),
        name=f"pair_finish_{first}",
    )(*operands)


def on_device(
    atoms,
    pair,
    token_atoms,
    attn_bias,
    w_attn,
    w_attn_out,
    w_single,
    w_pair_left,
    w_pair_right,
    w_atom_back,
    w_tri_in,
    w_tri_gate,
    w_tri_out,
):
    rows, cols = lax.axis_size("row"), lax.axis_size("col")
    channels, tile_rows, tile_cols = pair.shape
    atoms_out, lanes, sides = atom_stage(
        pair,
        atoms,
        token_atoms,
        attn_bias,
        w_attn,
        w_attn_out,
        w_single,
        w_pair_left,
        w_pair_right,
        w_atom_back,
    )
    tri_in = 0.5 * w_tri_in.T.reshape(4, channels, channels)
    right_weights = interleave(tri_in[2], tri_in[3])
    left_weights = interleave(tri_in[0], tri_in[1], 0.5 * w_tri_gate.T)
    hold = lax.optimization_barrier

    (right_a,) = front(lanes, sides, right_weights, RIGHT_FIRST, "right_first")
    right_a, lanes = hold((right_a, lanes))
    got_a = exchange(right_a)
    rights_b = RIGHT_SECOND[1] - RIGHT_SECOND[0]
    steps_b = rights_b + SECOND[1] - SECOND[0]
    (both_b,) = front(lanes, sides, right_weights, RIGHT_SECOND, "right_second", 0, steps_b)
    both_b, gate_1 = front(
        lanes, sides, left_weights, SECOND, "left_second", rights_b, steps_b, both_b
    )
    both_b, lanes, got_a = hold((both_b, lanes, got_a))
    got_b = exchange(both_b)
    left_0, gate_0 = front(lanes, sides, left_weights, FIRST, "left_first")
    left_0, got_b = hold((left_0, got_b))
    got_left_0 = exchange(left_0)
    rights = (got_a, got_b)
    right_at = (slice(0, got_a.shape[1]), slice(0, rights_b * ROWS_PER_STEP))
    left_at = slice(rights_b * ROWS_PER_STEP, steps_b * ROWS_PER_STEP)
    products_1 = triangle(got_b, left_at, rights, right_at, rows, cols, "triangle_second")
    products_1, got_left_0 = hold((products_1, got_left_0))
    back_1 = exchange(products_1)
    left_at = slice(0, got_left_0.shape[1])
    products_0 = triangle(got_left_0, left_at, rights, right_at, rows, cols, "triangle_first")
    products_0, back_1 = hold((products_0, back_1))
    back_0 = exchange(products_0)
    out_weights = w_tri_out.T
    pair_out = finish(back_1, gate_1, pair, sides, out_weights, SECOND, None)
    pair_out = finish(back_0, gate_0, pair, sides, out_weights, FIRST, pair_out)
    return (atoms_out, pair_out)


def solution(mesh):
    in_specs = (
        P(("row", "col"), None),
        P(None, "row", "col"),
        P(),
        P(("row", "col"), None, None, None),
        P(),
        P(),
        P(),
        P(),
        P(),
        P(),
        P(),
        P(),
        P(),
    )
    out_specs = (P(("row", "col"), None), P(None, "row", "col"))
    return jax.shard_map(
        on_device, mesh=mesh, in_specs=in_specs, out_specs=out_specs, check_vma=False
    )
```

time: 897 us -> 430 us (0.48)
  blocking collectives: 216 us -> 0 us
  Pallas kernels: 0 us -> 117 us
  matrix products: 106 us -> 0 us
  waiting for transfers between devices: 343 us -> 247 us
  local copies, waits for them, and re-layouts: 94.7 us -> 5.37 us
  other arithmetic: 73.5 us -> 0.95 us
  starting transfers between devices: 42.5 us -> 56.3 us
  between operations: 14.6 us -> 0.83 us
    all_gather x3 -> x0, blocking collectives: 216 us -> none  [the longest x1 146 us: on_device(): lax.all_gather(back_proj, ('row', 'col'), axis=0, tiled=True)]
    reduce_scatter x1 -> x0, waiting for transfers between devices: 195 us -> none  [on_device(): lax.psum_scatter(lax.dot_general(one_hot, hidden, (((0,), (0,)), ((), ())...]
    pallas_call x0 -> x13, Pallas kernels: none -> 117 us  [the longest x4 40.9 us: front(): pl.pallas_call(functools.partial(front_kernel, parts), grid=(steps,), out...]
    dot_general x14 -> x0, matrix products: 106 us -> none  [the longest x1 27.1 us: on_device(): jnp.einsum('cij,cd->dij', tri_norm, w_tri_out, preferred_element_type=jnp...]
    all_to_all x3 -> x7, waiting for transfers between devices: 148 us -> 246 us  [exchange(): lax.all_to_all(blocks, MESH_AXES, split_axis=0, concat_axis=0, tiled=True)]
    reshape x5 -> x0, local copies, waits for them, and re-layouts: 33.2 us -> none  [the longest x1 12.2 us: on_device(): factor_left.reshape(channels, 1, tile_rows, tile_cols)]
    unnamed x23 -> x13, local copies, waits for them, and re-layouts: 35.2 us -> 3.18 us
    reduce_sum x7 -> x0, other arithmetic: 30.9 us -> none  [the longest x3 17.4 us: layer_norm(): variance = jnp.mean(centred * centred, axis=along, keepdims=True)]
  transfers between devices with their start and end apart: 6 -> 9, of which waited for: 3 -> 9; matrix products, arithmetic and copies ran while one was open for 10% -> 1% of each run, Pallas kernels for 0% -> 20%
where the time goes in v1:
time: 430 us; the launch traced here: 428 us
  waiting for transfers between devices  247 us (57%)
  Pallas kernels  117 us (27%)
  starting transfers between devices  56.3 us (13%)
  local copies, waits for them, and re-layouts  5.37 us (1%)
    all_to_all x7, waiting for transfers between devices, exchange(): lax.all_to_all(blocks, MESH_AXES, split_axis=0, concat_axis=0, tiled=True)  246 us
    all_to_all x7, starting transfers between devices, exchange(): lax.all_to_all(blocks, MESH_AXES, split_axis=0, concat_axis=0, tiled=True)  45.1 us
    pallas_call x4, Pallas kernels, front(): pl.pallas_call(functools.partial(front_kernel, parts), grid=(steps,), out...  40.9 us
    pallas_call x2, Pallas kernels, triangle(): pl.pallas_call(functools.partial(triangle_kernel, left_at, right_at), gri...  30.8 us
    pallas_call x2, Pallas kernels, finish(): pl.pallas_call(finish_kernel, grid=(steps,), out_shape=jax.ShapeDtypeStru...  24.9 us
    pallas_call x2, Pallas kernels, to_lanes(): pl.pallas_call(lanes_kernel, grid=(steps,), out_shape=jax.ShapeDtypeStruc...  12.9 us
  transfers between devices with their start and end apart: 9, of which 9 were waited for; matrix products, arithmetic and copies ran while one was open for 1% of the time, Pallas kernels for 20%

profile of v1, /device:TPU:1, one launch (start us, length us, event | category | flops | bytes accessed | tf_op | source)
XLA Modules:
  0.0 428.1 jit_solution(15651416188524818686)
XLA Ops:
  6.7 6.8 %collective-permute-start.1 = (f32[208,128]{1,0:T(8,128)S(1)}, f32[208,128]{1,0:T(8,128)S(1)}, u32[]{:S(2)}, u32[]{:S(2)}) collective-permute-start(f32[208,128]{1,0:T(8,128)S(1)} %pad_maximum_fusion.1), channel_id=1, source_target_pairs={{1,0},{2,1},{3,2},{4,3},{5,4},{6,5},{7,6},{8,7},{9,8},{10,9},{11,1... | collective-permute-start | bytes 319496 | tf_op jit(solution)/shard_map/ppermute | solution.py:261
  15.9 6.2 %atom_attention.1 = (bf16[128,128]{1,0:T(8,128)(2,1)}, bf16[128,16,128]{2,1,0:T(8,128)(2,1)}) custom-call(s32[1]{0:T(128)} %bitcast.first_ref, f32[208,128]{1,0:T(8,128)} %copy-done.3, f32[208,128]{1,0:T(8,128)} %copy-done.4, s32[16,128]{1,0:T(8,128)} %bitcast.39, bf16[128,128]{1,0:T(8,128)(2,1)} %refs_0_.1, bf16[128,512]{1,0:T(8,128)(2,1)} %refs_1_.1, ...), custom_call_target="tpu_custom_call" | custom-call | flops 400000000 | bytes 3000000 | tf_op jit(solution)/shard_map/atom_attention/pallas_call | solution.py:279
  22.1 10.9 %all-to-all-start = ((bf16[128,16,128]{2,1,0:T(8,128)(2,1)}), bf16[128,16,128]{2,1,0:T(8,128)(2,1)S(1)}, u32[]{:S(2)}, u32[]{:S(2)}) async-start(bf16[128,16,128]{2,1,0:T(8,128)(2,1)} %get-tuple-element.29), calls=%async_computation | async-start | bytes 1048576 | tf_op jit(solution)/shard_map/all_to_all | solution.py:233
  34.0 6.5 %pair_lanes_0.1.rest_0_ = bf16[128,32768]{1,0:T(8,128)(2,1)} custom-call(bf16[128,256,128]{2,1,0:T(8,128)(2,1)} %pair_ref.5), custom_call_target="tpu_custom_call" | custom-call | bytes 8388608 | tf_op jit(solution)/shard_map/pair_lanes_0/pallas_call | solution.py:365
  40.5 5.9 %all-to-all-done.got_ref = bf16[128,16,128]{2,1,0:T(8,128)(2,1)S(1)} async-done(((bf16[128,16,128]{2,1,0:T(8,128)(2,1)}), bf16[128,16,128]{2,1,0:T(8,128)(2,1)S(1)}, u32[]{:S(2)}, u32[]{:S(2)}) %all-to-all-start) | async-done | bytes 524320 | tf_op jit(solution)/shard_map/all_to_all | solution.py:233
  52.8 6.5 %pair_lanes_4.1.pair_ref = bf16[128,32768]{1,0:T(8,128)(2,1)} custom-call(bf16[128,256,128]{2,1,0:T(8,128)(2,1)} %pair_ref.5, bf16[128,32768]{1,0:T(8,128)(2,1)} %pair_lanes_0.1.rest_0_), custom_call_target="tpu_custom_call", output_to_operand_aliasing={{}: (1, {})} | custom-call | bytes 8388608 | tf_op jit(solution)/shard_map/pair_lanes_4/pallas_call | solution.py:365
  59.3 6.3 %all-to-all-done.1.got_ref = bf16[128,16,128]{2,1,0:T(8,128)(2,1)S(1)} async-done(((bf16[128,16,128]{2,1,0:T(8,128)(2,1)}), bf16[128,16,128]{2,1,0:T(8,128)(2,1)S(1)}, u32[]{:S(2)}, u32[]{:S(2)}) %all-to-all-start.1) | async-done | bytes 524320 | tf_op jit(solution)/shard_map/all_to_all | solution.py:233
  67.0 11.2 %right_first.1 = bf16[128,160,128]{2,1,0:T(8,128)(2,1)} custom-call(bf16[128,32768]{1,0:T(8,128)(2,1)} %pair_lanes_4.1.pair_ref, f32[384,128]{1,0:T(8,128)} %copy-done, f32[384,128]{1,0:T(8,128)} %copy-done, bf16[256,128]{1,0:T(8,128)(2,1)} %bitcast.32), custom_call_target="tpu_custom_call" | custom-call | flops 1342177280 | bytes 10485760 | tf_op jit(solution)/shard_map/right_first/pallas_call | solution.py:458
  78.2 6.0 %all-to-all-start.2 = ((bf16[128,160,128]{2,1,0:T(8,128)(2,1)}), bf16[128,160,128]{2,1,0:T(8,128)(2,1)}, u32[]{:S(2)}, u32[]{:S(2)}) async-start(bf16[128,160,128]{2,1,0:T(8,128)(2,1)} %right_first.1), calls=%async_computation.2 | async-start | bytes 10485760 | tf_op jit(solution)/shard_map/all_to_all | solution.py:233
  85.0 7.6 %right_second.1.rest_0_ = bf16[128,224,128]{2,1,0:T(8,128)(2,1)} custom-call(bf16[128,32768]{1,0:T(8,128)(2,1)} %pair_lanes_4.1.pair_ref, f32[384,128]{1,0:T(8,128)} %copy-done, f32[384,128]{1,0:T(8,128)} %copy-done, bf16[256,128]{1,0:T(8,128)(2,1)} %bitcast.33), custom_call_target="tpu_custom_call" | custom-call | flops 805306368 | bytes 6291456 | tf_op jit(solution)/shard_map/right_second/pallas_call | solution.py:458
  92.5 11.1 %left_second.1 = (bf16[128,224,128]{2,1,0:T(8,128)(2,1)}, bf16[128,16384]{1,0:T(8,128)(2,1)}) custom-call(bf16[128,32768]{1,0:T(8,128)(2,1)} %pair_lanes_4.1.pair_ref, f32[384,128]{1,0:T(8,128)} %copy-done, f32[384,128]{1,0:T(8,128)} %copy-done, bf16[384,128]{1,0:T(8,128)(2,1)} %bitcast.30, ...), custom_call_target="tpu_custom_call", output_to_operand_aliasing={{0}: (4, {})} | custom-call | flops 1610612736 | bytes 12582912 | tf_op jit(solution)/shard_map/left_second/pallas_call | solution.py:458
  103.6 44.2 %all-to-all-done.2.refs_0_ = bf16[128,160,128]{2,1,0:T(8,128)(2,1)} async-done(((bf16[128,160,128]{2,1,0:T(8,128)(2,1)}), bf16[128,160,128]{2,1,0:T(8,128)(2,1)}, u32[]{:S(2)}, u32[]{:S(2)}) %all-to-all-start.2) | async-done | bytes 5242912 | tf_op jit(solution)/shard_map/all_to_all | solution.py:233
  147.8 5.2 %all-to-all-start.3 = ((bf16[128,224,128]{2,1,0:T(8,128)(2,1)}), bf16[128,224,128]{2,1,0:T(8,128)(2,1)}, u32[]{:S(2)}, u32[]{:S(2)}) async-start(bf16[128,224,128]{2,1,0:T(8,128)(2,1)} %get-tuple-element.42), calls=%async_computation.3 | async-start | bytes 14680064 | tf_op jit(solution)/shard_map/all_to_all | solution.py:233
  153.0 11.0 %left_first.1 = (bf16[128,128,128]{2,1,0:T(8,128)(2,1)}, bf16[128,16384]{1,0:T(8,128)(2,1)}) custom-call(bf16[128,32768]{1,0:T(8,128)(2,1)} %pair_lanes_4.1.pair_ref, f32[384,128]{1,0:T(8,128)} %copy-done, f32[384,128]{1,0:T(8,128)} %copy-done, bf16[384,128]{1,0:T(8,128)(2,1)} %bitcast.31), custom_call_target="tpu_custom_call" | custom-call | flops 1610612736 | bytes 12582912 | tf_op jit(solution)/shard_map/left_first/pallas_call | solution.py:458
  164.0 76.6 %all-to-all-done.3.refs_1_ = bf16[128,224,128]{2,1,0:T(8,128)(2,1)} async-done(((bf16[128,224,128]{2,1,0:T(8,128)(2,1)}), bf16[128,224,128]{2,1,0:T(8,128)(2,1)}, u32[]{:S(2)}, u32[]{:S(2)}) %all-to-all-start.3) | async-done | bytes 7340064 | tf_op jit(solution)/shard_map/all_to_all | solution.py:233
  240.7 8.2 %all-to-all-start.4 = ((bf16[128,128,128]{2,1,0:T(8,128)(2,1)}), bf16[128,128,128]{2,1,0:T(8,128)(2,1)}, u32[]{:S(2)}, u32[]{:S(2)}) async-start(bf16[128,128,128]{2,1,0:T(8,128)(2,1)} %get-tuple-element.45), calls=%async_computation.4 | async-start | bytes 8388608 | tf_op jit(solution)/shard_map/all_to_all | solution.py:233
  248.9 15.9 %triangle_second.1 = bf16[8,16,128,128]{3,2,1,0:T(8,128)(2,1)} custom-call(bf16[8,16,224,128]{3,2,1,0:T(8,128)(2,1)} %bitcast.16.left_ref, bf16[128,160,128]{2,1,0:T(8,128)(2,1)} %all-to-all-done.2.refs_0_, bf16[128,224,128]{2,1,0:T(8,128)(2,1)} %all-to-all-done.3.refs_1_), custom_call_target="tpu_custom_call" | custom-call | flops 8589934592 | bytes 16777216 | tf_op jit(solution)/shard_map/triangle_second/pallas_call | solution.py:506
  264.8 36.2 %all-to-all-done.4 = bf16[128,128,128]{2,1,0:T(8,128)(2,1)} async-done(((bf16[128,128,128]{2,1,0:T(8,128)(2,1)}), bf16[128,128,128]{2,1,0:T(8,128)(2,1)}, u32[]{:S(2)}, u32[]{:S(2)}) %all-to-all-start.4) | async-done | bytes 4194336 | tf_op jit(solution)/shard_map/all_to_all | solution.py:233
  306.1 14.9 %triangle_first.1 = bf16[8,16,128,128]{3,2,1,0:T(8,128)(2,1)} custom-call(bf16[8,16,128,128]{3,2,1,0:T(8,128)(2,1)} %bitcast.18.left_ref, bf16[128,160,128]{2,1,0:T(8,128)(2,1)} %all-to-all-done.2.refs_0_, bf16[128,224,128]{2,1,0:T(8,128)(2,1)} %all-to-all-done.3.refs_1_), custom_call_target="tpu_custom_call" | custom-call | flops 8589934592 | bytes 16777216 | tf_op jit(solution)/shard_map/triangle_first/pallas_call | solution.py:506
  320.9 37.4 %all-to-all-done.5.back_ref = bf16[128,128,128]{2,1,0:T(8,128)(2,1)} async-done(((bf16[128,128,128]{2,1,0:T(8,128)(2,1)}), bf16[128,128,128]{2,1,0:T(8,128)(2,1)}, u32[]{:S(2)}, u32[]{:S(2)}) %all-to-all-start.5) | async-done | bytes 4194336 | tf_op jit(solution)/shard_map/all_to_all | solution.py:233
  358.3 5.1 %all-to-all-start.6 = ((bf16[128,128,128]{2,1,0:T(8,128)(2,1)}), bf16[128,128,128]{2,1,0:T(8,128)(2,1)}, u32[]{:S(2)}, u32[]{:S(2)}) async-start(bf16[128,128,128]{2,1,0:T(8,128)(2,1)} %bitcast.28), calls=%async_computation.6 | async-start | bytes 8388608 | tf_op jit(solution)/shard_map/all_to_all | solution.py:233
  364.1 12.5 %pair_finish_4.1.rest_0_ = bf16[128,256,128]{2,1,0:T(8,128)(2,1)} custom-call(bf16[128,128,128]{2,1,0:T(8,128)(2,1)} %all-to-all-done.5.back_ref, bf16[128,16384]{1,0:T(8,128)(2,1)} %get-tuple-element.51.gate_ref, bf16[128,256,128]{2,1,0:T(8,128)(2,1)} %pair_ref.5, f32[384,128]{1,0:T(8,128)} %copy-done, f32[384,128]{1,0:T(8,128)} %copy-done, ...), custom_call_target="tpu_custom_call" | custom-call | flops 536870912 | bytes 16777216 | tf_op jit(solution)/shard_map/pair_finish_4/pallas_call | solution.py:581
  376.6 39.0 %all-to-all-done.6.back_ref = bf16[128,128,128]{2,1,0:T(8,128)(2,1)} async-done(((bf16[128,128,128]{2,1,0:T(8,128)(2,1)}), bf16[128,128,128]{2,1,0:T(8,128)(2,1)}, u32[]{:S(2)}, u32[]{:S(2)}) %all-to-all-start.6) | async-done | bytes 4194336 | tf_op jit(solution)/shard_map/all_to_all | solution.py:233
  415.6 12.4 %pair_finish_0.1 = bf16[128,256,128]{2,1,0:T(8,128)(2,1)} custom-call(bf16[128,128,128]{2,1,0:T(8,128)(2,1)} %all-to-all-done.6.back_ref, bf16[128,16384]{1,0:T(8,128)(2,1)} %get-tuple-element.49.gate_ref, bf16[128,256,128]{2,1,0:T(8,128)(2,1)} %pair_ref.5, f32[384,128]{1,0:T(8,128)} %copy-done, f32[384,128]{1,0:T(8,128)} %copy-done, ...), custom_call_target="tpu_custom_call", output_to_operand_aliasing={{}: (6, {})} | custom-call | flops 536870912 | bytes 16777216 | tf_op jit(solution)/shard_map/pair_finish_0/pallas_call | solution.py:581
  (32 shorter events, 23.8 us)
Async XLA Ops:
  2.3 12.3 %collective-permute-start = (f32[208,128]{1,0:T(8,128)S(1)}, f32[208,128]{1,0:T(8,128)S(1)}, u32[]{:S(2)}, u32[]{:S(2)}) collective-permute-start(f32[208,128]{1,0:T(8,128)S(1)} %pad_maximum_fusion), channel_id=1, source_target_pairs={{0,1},{1,2},{2,3},{3,4},{4,5},{5,6},{6,7},{7,8},{8,9},{9,10},{10,1... | collective-permute-start | bytes 319496 | tf_op jit(solution)/shard_map/ppermute | solution.py:258
  6.7 8.5 %collective-permute-start.1 = (f32[208,128]{1,0:T(8,128)S(1)}, f32[208,128]{1,0:T(8,128)S(1)}, u32[]{:S(2)}, u32[]{:S(2)}) collective-permute-start(f32[208,128]{1,0:T(8,128)S(1)} %pad_maximum_fusion.1), channel_id=1, source_target_pairs={{1,0},{2,1},{3,2},{4,3},{5,4},{6,5},{7,6},{8,7},{9,8},{10,9},{11,1... | collective-permute-start | bytes 319496 | tf_op jit(solution)/shard_map/ppermute | solution.py:261
  14.7 0.6 copy-start.3
  15.2 0.7 copy-start.4
  22.1 24.3 %all-to-all-start = ((bf16[128,16,128]{2,1,0:T(8,128)(2,1)}), bf16[128,16,128]{2,1,0:T(8,128)(2,1)S(1)}, u32[]{:S(2)}, u32[]{:S(2)}) async-start(bf16[128,16,128]{2,1,0:T(8,128)(2,1)} %get-tuple-element.29), calls=%async_computation | async-start | bytes 1048576 | tf_op jit(solution)/shard_map/all_to_all | solution.py:233
  47.3 18.2 %all-to-all-start.1 = ((bf16[128,16,128]{2,1,0:T(8,128)(2,1)}), bf16[128,16,128]{2,1,0:T(8,128)(2,1)S(1)}, u32[]{:S(2)}, u32[]{:S(2)}) async-start(bf16[128,16,128]{2,1,0:T(8,128)(2,1)} %spread_tokens.1), calls=%async_computation.1 | async-start | bytes 1048576 | tf_op jit(solution)/shard_map/all_to_all | solution.py:233
  66.3 0.7 copy-start
  78.2 6.0 %copy-start.1 = (bf16[128,128]{1,0:T(8,128)(2,1)S(1)}, bf16[128,128]{1,0:T(8,128)(2,1)}, u32[]{:S(2)}) copy-start(bf16[128,128]{1,0:T(8,128)(2,1)} %param.24) | copy-start | bytes 98308
  78.2 69.6 %all-to-all-start.2 = ((bf16[128,160,128]{2,1,0:T(8,128)(2,1)}), bf16[128,160,128]{2,1,0:T(8,128)(2,1)}, u32[]{:S(2)}, u32[]{:S(2)}) async-start(bf16[128,160,128]{2,1,0:T(8,128)(2,1)} %right_first.1), calls=%async_computation.2 | async-start | bytes 10485760 | tf_op jit(solution)/shard_map/all_to_all | solution.py:233
  147.8 92.8 %all-to-all-start.3 = ((bf16[128,224,128]{2,1,0:T(8,128)(2,1)}), bf16[128,224,128]{2,1,0:T(8,128)(2,1)}, u32[]{:S(2)}, u32[]{:S(2)}) async-start(bf16[128,224,128]{2,1,0:T(8,128)(2,1)} %get-tuple-element.42), calls=%async_computation.3 | async-start | bytes 14680064 | tf_op jit(solution)/shard_map/all_to_all | solution.py:233
  240.7 60.3 %all-to-all-start.4 = ((bf16[128,128,128]{2,1,0:T(8,128)(2,1)}), bf16[128,128,128]{2,1,0:T(8,128)(2,1)}, u32[]{:S(2)}, u32[]{:S(2)}) async-start(bf16[128,128,128]{2,1,0:T(8,128)(2,1)} %get-tuple-element.45), calls=%async_computation.4 | async-start | bytes 8388608 | tf_op jit(solution)/shard_map/all_to_all | solution.py:233
  301.0 57.3 %all-to-all-start.5 = ((bf16[128,128,128]{2,1,0:T(8,128)(2,1)}), bf16[128,128,128]{2,1,0:T(8,128)(2,1)}, u32[]{:S(2)}, u32[]{:S(2)}) async-start(bf16[128,128,128]{2,1,0:T(8,128)(2,1)} %bitcast.29), calls=%async_computation.5 | async-start | bytes 8388608 | tf_op jit(solution)/shard_map/all_to_all | solution.py:233
  320.9 42.5 %copy-start.2 = (bf16[128,128]{1,0:T(8,128)(2,1)S(1)}, bf16[128,128]{1,0:T(8,128)(2,1)}, u32[]{:S(2)}) copy-start(bf16[128,128]{1,0:T(8,128)(2,1)} %param.25) | copy-start | bytes 98308
  358.3 57.3 %all-to-all-start.6 = ((bf16[128,128,128]{2,1,0:T(8,128)(2,1)}), bf16[128,128,128]{2,1,0:T(8,128)(2,1)}, u32[]{:S(2)}, u32[]{:S(2)}) async-start(bf16[128,128,128]{2,1,0:T(8,128)(2,1)} %bitcast.28), calls=%async_computation.6 | async-start | bytes 8388608 | tf_op jit(solution)/shard_map/all_to_all | solution.py:233
